TPU v7x, 32 devices: a whole 2x2x4 slice. The times are simulated.
32 devices in a mesh: runs: 2 (over x), gy: 16 (over z, y, core).
Axes of the slice: x: 2, y: 2, z: 4, core: 2. Of those that a mesh axis runs over, the one named last changes fastest.
Arguments:
- depth: float32 [1024, 1920], P(('runs', 'gy')), parts along dimension 0, may hold values from 0.02 to 3
- flux_east: float32 [1024, 1920], P(('runs', 'gy')), parts along dimension 0, may hold values from -2 to 2
- flux_south: float32 [1024, 1920], P(('runs', 'gy')), parts along dimension 0, may hold values from -2 to 2
- river_section: float32 [4096], P(('runs', 'gy')), parts along dimension 0, may hold values from 0 to 2
- bed_level: float32 [512, 1920], P('gy'), may hold values from -3 to 3
- rough_class: int32 [512, 1920], P('gy'), may hold values from 0 to 7
- manning_table: float32 [8], replicated, may hold values from 0.02 to 0.15
- bank_cell: int32 [4, 2048], P(None, 'gy'), may hold values from 0 to 983039, as said below
Outputs:
- depth_out: float32 [1024, 1920], P(('runs', 'gy')), parts along dimension 0
- east_out: float32 [1024, 1920], P(('runs', 'gy')), parts along dimension 0
- south_out: float32 [1024, 1920], P(('runs', 'gy')), parts along dimension 0
- section_out: float32 [4096], P(('runs', 'gy')), parts along dimension 0
There are 2 independent parts, one for each index of `runs`. A program takes and returns all parts, laid end to end along the dimension named above; an argument that names none is the same for every part. Nothing has to cross between parts.
Inputs may be any that keep to these rules, and one draw needn't show every extreme that they name: `bank_cell`: the 4 corridor cells of a node are consecutive flat indices row * 1920 + column within one map row. Node n is owned by gy index o = n // 128, and all its corridor cells lie in map rows from max((o - 1) * 32, 0) to min((o + 2) * 32, 512) - 1.
All inputs are finite; a program needn't handle non-finite values.
Results may differ from a plain program's by a relative error of at most 0.00013.
Values sent between devices are 32-bit elements; how exact they have to be, the bound alone decides.
No kernel may reach another device: no remote copies, remote signals or barrier semaphores. Data moves between devices by JAX's collectives and lax.ppermute only.
A program may use at most 64 MiB of HBM per device.

v0:
```python
import functools

import jax
import jax.numpy as jnp
from jax import lax
from jax.experimental import pallas as pl
from jax.experimental.pallas import tpu as pltpu
from jax.sharding import PartitionSpec as P

STEPS = 4

GRAV = 9.81
TSTEP = 8.0
CELL = 90.0
FLOOR = 0.05
BANK_COEF = 200.0
CELL_AREA = 8100.0
NODE_AREA = 20000.0

LANES = 128
HALO = 4
SLOPE = GRAV * TSTEP / CELL
SPREAD = TSTEP / CELL
FEED = TSTEP * BANK_COEF / CELL_AREA
DRAIN = TSTEP * BANK_COEF / NODE_AREA
VMEM_LIMIT = 32 * 1024 * 1024

VMEM_SPEC = pl.BlockSpec(memory_space=pltpu.VMEM)
HBM_SPEC = pl.BlockSpec(memory_space=pltpu.HBM)


def swapped(value, first):
    count = lax.axis_size("gy")
    pairs = []
    for low in range(first, count - 1, 2):
        pairs += [(low, low + 1), (low + 1, low)]
    return lax.ppermute(value, "gy", pairs)


def cols(chunk):
    return slice(chunk * LANES, (chunk + 1) * LANES)


def lanes_of(rows):
    return lax.broadcasted_iota(jnp.int32, (rows, LANES), 1)


def moved_left(value, following, by):
    return jnp.where(
        lanes_of(value.shape[0]) >= LANES - by,
        pltpu.roll(following, LANES - by, 1),
        pltpu.roll(value, LANES - by, 1),
    )


def moved_up(value):
    return pltpu.roll(value, value.shape[0] - 1, 0)


def split3(value):
    high = value.astype(jnp.bfloat16)
    rest = value - high.astype(jnp.float32)
    middle = rest.astype(jnp.bfloat16)
    low = (rest - middle.astype(jnp.float32)).astype(jnp.bfloat16)
    return high, middle, low


def one_hot(count, key):
    rows = lax.broadcasted_iota(jnp.int32, (count, key.shape[1]), 0)
    return jnp.where(rows == key, 1.0, 0.0)


def drag_of(mann_a, mann_b):
    pair = mann_a + mann_b
    return (0.25 * GRAV * TSTEP) * (pair * pair)


def looked_up(klass, entries):
    value = jnp.broadcast_to(entries[0], klass.shape)
    for k in range(1, len(entries)):
        value = jnp.where(klass == k, entries[k], value)
    return value


def face(flux, surf_a, surf_b, bed_max, drag):
    flow_depth = jnp.maximum(jnp.maximum(surf_a, surf_b) - bed_max, FLOOR)
    power = jnp.exp2((-7.0 / 3.0) * jnp.log2(flow_depth))
    driven = flux - SLOPE * flow_depth * (surf_b - surf_a)
    damping = 1.0 + drag * jnp.abs(flux) * power
    return driven * pl.reciprocal(damping, approx=True)


def window_sums(blocks, reach, forward):
    height = blocks[0].shape[0]
    count = len(blocks)
    spare = -(count * height) % 16
    whole = blocks + ([jnp.zeros((spare, LANES), jnp.float32)] if spare else [])
    whole = jnp.concatenate(whole, axis=0)
    high = whole.astype(jnp.bfloat16)
    low = (whole - high.astype(jnp.float32)).astype(jnp.bfloat16)
    source = lax.broadcasted_iota(jnp.int32, (2 * LANES, 2 * LANES), 0) % LANES
    target = lax.broadcasted_iota(jnp.int32, (2 * LANES, 2 * LANES), 1)
    spill = target >= LANES
    target = target % LANES
    if forward:
        ahead = source - target + jnp.where(spill, LANES, 0)
    else:
        ahead = target - source + jnp.where(spill, LANES, 0)
    band = jnp.where((ahead >= 0) & (ahead < reach), 1.0, 0.0).astype(jnp.bfloat16)
    sums = jnp.dot(
        jnp.concatenate([high, low], axis=1), band, preferred_element_type=jnp.float32
    )
    results = []
    for block in range(count):
        result = sums[block * height : (block + 1) * height, :LANES]
        beside = block + 1 if forward else block - 1
        if 0 <= beside < count:
            result = result + sums[beside * height : (beside + 1) * height, LANES:]
        results.append(result)
    return results


def east_walled(value, chunk, chunks):
    if chunk + 1 < chunks:
        return value
    return jnp.where(lanes_of(value.shape[0]) == LANES - 1, 0.0, value)


def located(cell, position, rows, ext, columns):
    base = ((position * rows - HALO) * columns + 1).astype(jnp.float32)
    offset = cell - base
    valid = (cell > 0.0) & (offset >= 0.0) & (offset < float(ext * columns))
    offset = jnp.where(valid, offset, 0.0)
    row = jnp.floor((offset + 0.5) * (1.0 / columns))
    column = (offset - row * float(columns)).astype(jnp.int32)
    row = row.astype(jnp.int32) - HALO
    row = jnp.where(row < 0, row + ext, row)
    chunk = column // LANES
    return valid, row, chunk, column - chunk * LANES


def scattered(section, key, lane, count):
    at_lane = one_hot(LANES, lane)
    parts = [at_lane] + [at_lane * part.astype(jnp.float32) for part in split3(section)]
    grid = lax.dot_general(
        one_hot(-(-count // 16) * 16, key).astype(jnp.bfloat16),
        jnp.concatenate(parts, axis=0).astype(jnp.bfloat16),
        (((1,), (1,)), ((), ())),
        preferred_element_type=jnp.float32,
    )
    number = grid[:, :LANES]
    total = (grid[:, LANES : 2 * LANES] + grid[:, 2 * LANES : 3 * LANES]) + grid[:, 3 * LANES :]
    return number, total


def pack_kernel(
    depth, bed, rough, east, south, section, cells, to_other, own, held, held_rough, held_cells, sems
):
    rows, columns = depth.shape
    even = lax.axis_index("gy") % 2 == 0
    start = pl.multiple_of(jnp.where(even, 0, rows - 8), 8)
    copies = [
        pltpu.make_async_copy(source, target, sems.at[slot])
        for slot, (source, target) in enumerate(
            (
                (depth.at[pl.ds(start, 8), :], held.at[0]),
                (bed.at[pl.ds(start, 8), :], held.at[1]),
                (rough.at[pl.ds(start, 8), :], held_rough),
                (east.at[pl.ds(start, 8), :], held.at[2]),
                (south.at[pl.ds(start, 8), :], held.at[3]),
                (section, own.at[pl.ds(0, 1), :]),
                (cells, held_cells),
            )
        )
    ]
    for copy in copies:
        copy.start()
    for slot in range(5):
        copies[slot].wait()
        block = (
            held_rough[...].astype(jnp.float32) if slot == 2 else held[slot - (slot > 2)]
        )
        to_other[slot] = jnp.where(even, block[:HALO], block[8 - HALO :])
    for copy in copies[5:]:
        copy.wait()
    own[1:2, :] = (held_cells[0:1, :] + 1).astype(jnp.float32)


def join_kernel(before, own, section, cells, to_other):
    even = lax.axis_index("gy") % 2 == 0
    owned = own.shape[1]
    rows = (own[0:1, :], own[1:2, :], section[...], (cells[0:1, :] + 1).astype(jnp.float32))

    def put(spare):
        for slot, row in enumerate(rows):
            to_other[3, spare : spare + 1, slot * owned : (slot + 1) * owned] = row

    @pl.when(even)
    def _():
        put(HALO - 1)

    @pl.when(jnp.logical_not(even))
    def _():
        put(0)


def picking(reach, rows, key, lane, takes, masks):
    for block in range(key.shape[1] // LANES):
        mine = slice(block * LANES, (block + 1) * LANES)

        def column(row):
            wide = jnp.broadcast_to(row[:, mine].astype(jnp.float32), (LANES, LANES))
            return jnp.transpose(wide).astype(jnp.int32)

        spread = lanes_of(LANES)
        at = column(key)
        after = jnp.where(at < 0, at, at + rows)
        for first in range(0, takes.shape[2], LANES):
            for half, place in enumerate((at, after)):
                hit = jnp.where(spread + first == place, 1.0, 0.0)
                takes[half, mine, first : first + LANES] = hit.astype(jnp.bfloat16)
        ahead = spread - column(lane)
        masks[0, mine, :] = jnp.where((ahead >= 0) & (ahead < reach), 1.0, 0.0)
        masks[1, mine, :] = jnp.where(ahead + LANES < reach, 1.0, 0.0)


def load_kernel(
    depth_in, east_in, south_in, bed_in, rough_in, table_in, *refs
):
    to_partner, surf, east, south, bed, rough, table_rows, table, sems = refs
    rows, columns = depth_in.shape
    even = lax.axis_index("gy") % 2 == 0
    own = pl.ds(0, rows)
    copies = [
        pltpu.make_async_copy(source, target.at[own, :], sems.at[slot])
        for slot, (source, target) in enumerate(
            (
                (depth_in, surf),
                (bed_in, bed),
                (rough_in, rough),
                (east_in, east),
                (south_in, south),
            )
        )
    ]
    copies.append(pltpu.make_async_copy(table_in, table, sems.at[5]))
    for copy in copies:
        copy.start()
    copies[5].wait()
    for k in range(table_rows.shape[0]):
        table_rows[k : k + 1, :] = jnp.broadcast_to(table[:, k : k + 1], (1, LANES))
    for slot, source in enumerate((surf, bed, rough, east, south)):
        copies[slot].wait()
        for chunk in range(columns // LANES):
            at = cols(chunk)
            first = source[:8, at].astype(jnp.float32)
            last = source[rows - 8 : rows, at].astype(jnp.float32)
            to_partner[slot, :, at] = jnp.where(even, last[8 - HALO :], first[:HALO])


def relay_kernel(by_other, prepared, near, beyond):
    del prepared
    even = lax.axis_index("gy") % 2 == 0
    owned = near.shape[1]
    for target, first in ((near, 0), (beyond, 2)):
        for slot in range(2):
            mine = slice((first + slot) * owned, (first + slot + 1) * owned)
            target[slot : slot + 1, :] = jnp.where(
                even, by_other[3, 0:1, mine], by_other[3, HALO - 1 : HALO, mine]
            )


def prepare_kernel(reach, table_rows, rough, own, partner_section, partner_cells, *refs):
    surf, east, south, bed = refs[4:8]
    mann, bed_e, bed_s, drag_e, drag_s, number, total, takes, masks = refs[8:]
    ext, columns = surf.shape
    rows = ext - 2 * HALO
    chunks = columns // LANES
    tiles = lax.axis_size("gy")
    position = lax.axis_index("gy")
    side = jnp.where(position % 2 == 0, 1, -1)
    entries = [table_rows[k : k + 1, :] for k in range(table_rows.shape[0])]
    for chunk in range(chunks):
        at = cols(chunk)
        mann[:rows, at] = looked_up(rough[:, at], entries)
        surf[:rows, at] = surf[:rows, at] + bed[:rows, at]

    partner = jnp.where(position + side < tiles, partner_cells[0:1, :] + 1, 0).astype(jnp.float32)
    section = jnp.concatenate([own[0:1, :], partner_section[...]], axis=1)
    cell = jnp.concatenate([own[1:2, :], partner], axis=1)
    valid, node_row, node_chunk, node_lane = located(cell, position, rows, ext, columns)
    key = jnp.where(valid, node_chunk * ext + node_row, -1)
    starts, levels = scattered(section, key, node_lane, chunks * ext)
    for chunk in range(chunks):
        at = cols(chunk)
        number[:, at] = starts[chunk * ext : (chunk + 1) * ext]
        total[:, at] = levels[chunk * ext : (chunk + 1) * ext]

    key = jnp.where(valid & (node_row < rows), node_chunk * rows + node_row, -1)
    picking(reach, rows, key, node_lane, takes, masks)

    kept = lax.broadcasted_iota(jnp.int32, (rows, LANES), 0) == rows - 1
    for chunk in range(chunks):
        at, then = cols(chunk), cols(min(chunk + 1, chunks - 1))
        s0, b0, m0 = surf[:rows, at], bed[:rows, at], mann[:rows, at]
        bed_max = jnp.maximum(b0, moved_left(b0, bed[:rows, then], 1))
        drag = drag_of(m0, moved_left(m0, mann[:rows, then], 1))
        bed_e[:rows, at] = bed_max
        drag_e[:rows, at] = drag
        new_east = face(
            east[:rows, at], s0, moved_left(s0, surf[:rows, then], 1), bed_max, drag
        )
        east[:rows, at] = east_walled(new_east, chunk, chunks)
        bed_max = jnp.maximum(b0, moved_up(b0))
        drag = drag_of(m0, moved_up(m0))
        bed_s[:rows, at] = bed_max
        drag_s[:rows, at] = drag
        q0 = south[:rows, at]
        south[:rows, at] = jnp.where(kept, q0, face(q0, s0, moved_up(s0), bed_max, drag))


def wall_of(ext, tiles):
    position = lax.axis_index("gy")
    rows = ext - 2 * HALO
    row = lax.broadcasted_iota(jnp.int32, (16, LANES), 0) + (ext - 16)
    return ((row == ext - 1) & (position == 0)) | ((row == rows - 1) & (position == tiles - 1))


def border_kernel(reach, tiles, by_partner, by_other, table_rows, near, beyond, *refs):
    surf, east, south, bed, mann, bed_e, bed_s, drag_e, drag_s, number, total, takes, masks = refs[11:]
    ext, columns = surf.shape
    rows = ext - 2 * HALO
    chunks = columns // LANES
    position = lax.axis_index("gy")
    even = position % 2 == 0
    entries = [table_rows[k : k + 1, :] for k in range(table_rows.shape[0])]
    row = lax.broadcasted_iota(jnp.int32, (2 * HALO, LANES), 0)
    spare = jnp.where(even, HALO, HALO - 1)
    for chunk in range(chunks):
        at = cols(chunk)
        halos = []
        for slot in range(5):
            a, b = by_partner[slot, :, at], by_other[slot, :, at]
            below = jnp.where(even, a, b)
            above = jnp.where(even, b, a)
            halos.append(jnp.concatenate([below, above], axis=0))
        surf[rows:, at] = halos[0] + halos[1]
        bed[rows:, at] = halos[1]
        mann[rows:, at] = looked_up(halos[2].astype(jnp.int32), entries)
        east[rows:, at] = jnp.where(row == spare, 0.0, halos[3])
        south[rows:, at] = halos[4]

    section = jnp.concatenate([near[0:1, :], beyond[0:1, :]], axis=1)
    cell = jnp.concatenate([near[1:2, :], beyond[1:2, :]], axis=1)
    valid, node_row, node_chunk, node_lane = located(cell, position, rows, ext, columns)
    key = jnp.where(valid, node_chunk * ext + node_row, -1)
    starts, levels = scattered(section, key, node_lane, chunks * ext)

    key = jnp.where(valid & (node_row < rows), node_chunk * rows + node_row, -1)
    owned = near.shape[1]
    picking(reach, rows, key[:, :owned], node_lane[:, :owned], takes, masks)

    wall = wall_of(ext, tiles)
    kept = lax.broadcasted_iota(jnp.int32, (16, LANES), 0) < 7
    for chunk in range(chunks):
        at, then = cols(chunk), cols(min(chunk + 1, chunks - 1))
        number[:, at] += starts[chunk * ext : (chunk + 1) * ext]
        total[:, at] += levels[chunk * ext : (chunk + 1) * ext]
        s0, b0, m0 = surf[rows:, at], bed[rows:, at], mann[rows:, at]
        bed_max = jnp.maximum(b0, moved_left(b0, bed[rows:, then], 1))
        drag = drag_of(m0, moved_left(m0, mann[rows:, then], 1))
        bed_e[rows:, at] = bed_max
        drag_e[rows:, at] = drag
        new_east = face(
            east[rows:, at], s0, moved_left(s0, surf[rows:, then], 1), bed_max, drag
        )
        east[rows:, at] = east_walled(new_east, chunk, chunks)

        def rolled_up(ref):
            value = jnp.concatenate([ref[rows - 8 :, at], ref[:8, at]], axis=0)
            return value[:16], moved_up(value)[:16]

        s0, s1 = rolled_up(surf)
        b0, b1 = rolled_up(bed)
        m0, m1 = rolled_up(mann)
        bed_max = jnp.maximum(b0, b1)
        drag = drag_of(m0, m1)
        bed_s[rows - 8 :, at] = bed_max
        drag_s[rows - 8 :, at] = drag
        q0 = south[rows - 8 :, at]
        new_south = jnp.where(wall, 0.0, face(q0, s0, s1, bed_max, drag))
        south[rows - 8 :, at] = jnp.where(kept, q0, new_south)


def fluxes(mine, wall, before, faces, east_out, south_out=None):
    surf, east, south = before
    bed_e, bed_s, drag_e, drag_s = faces
    chunks = surf.shape[1] // LANES
    rolled = pltpu.roll(surf[mine, cols(0)], LANES - 1, 1)
    lane = lanes_of(rolled.shape[0])
    for chunk in range(chunks):
        at = cols(chunk)
        s0 = surf[mine, at]
        rolled_then = rolled
        if chunk + 1 < chunks:
            rolled_then = pltpu.roll(surf[mine, cols(chunk + 1)], LANES - 1, 1)
        left = jnp.where(lane >= LANES - 1, rolled_then, rolled)
        rolled = rolled_then
        new_east = face(east[mine, at], s0, left, bed_e[mine, at], drag_e[mine, at])
        east_out[mine, at] = east_walled(new_east, chunk, chunks)
        if south_out is not None:
            s0 = surf[:, at]
            new_south = face(south[:, at], s0, moved_up(s0), bed_s[:, at], drag_s[:, at])
            south_out[:, at] = jnp.concatenate(
                [new_south[:-16], jnp.where(wall, 0.0, new_south[-16:])], axis=0
            )


def settled(mine, surf, east, south, gain):
    ext, columns = surf.shape
    rolled = 0.0
    for chunk in range(columns // LANES):
        at = cols(chunk)
        new_east = east[mine, at]
        new_south = south[:, at]
        lane = lanes_of(new_east.shape[0])
        rolled_before, rolled = rolled, pltpu.roll(new_east, 1, 1)
        west = jnp.where(lane < 1, rolled_before, rolled)
        north = pltpu.roll(new_south, 1, 0)[mine]
        inflow = west + north
        s0 = surf[mine, at]
        outflow = new_east + new_south[mine]
        yield chunk, s0 + (SPREAD * (inflow - outflow) + gain(chunk, s0))


def exchange(corridor, mine, surf, total, count, covers, total_out):
    chunks = surf.shape[1] // LANES
    sums = window_sums([total[mine, cols(chunk)] for chunk in range(chunks)], corridor, False)
    if total_out is not None:
        windows = window_sums([surf[mine, cols(chunk)] for chunk in range(chunks)], corridor, True)
        for chunk in range(chunks):
            at = cols(chunk)
            kept = (1.0 - corridor * DRAIN) * total[mine, at]
            total_out[mine, at] = kept + count[mine, at] * windows[chunk]

    def gain(chunk, value):
        return sums[chunk] - covers[mine, cols(chunk)] * value

    return gain


def given(corridor, surf, before, after):
    rows = surf.shape[0] - 2 * HALO
    for chunk in range(surf.shape[1] // LANES):
        at = cols(chunk)
        value = (DRAIN * (1.0 - corridor * DRAIN)) * surf[:rows, at]
        if before is not None:
            value = (1.0 - corridor * DRAIN) * before[:, at] + value
        after[:, at] = value


def first_kernel(corridor, surf, east, south, number, total, *refs):
    surf_1, total_1, count, covers, given_1, total_0 = refs
    rows = surf.shape[0] - 2 * HALO
    chunks = surf.shape[1] // LANES
    own = slice(0, rows)
    covering = window_sums([number[own, cols(chunk)] for chunk in range(chunks)], corridor, False)
    for chunk in range(chunks):
        at = cols(chunk)
        count[own, at] = (FEED * DRAIN) * number[own, at]
        covers[own, at] = FEED * covering[chunk]
        total_0[own, at] = FEED * total[own, at]
    gain = exchange(corridor, own, surf, total_0, count, covers, total_1)
    for chunk, new_surf in settled(own, surf, east, south, gain):
        surf_1[own, cols(chunk)] = new_surf
    given(corridor, surf, None, given_1)


def second_kernel(corridor, tiles, far, surf, east, south, *refs):
    faces = refs[:4]
    number, total, given_1 = refs[4:7]
    surf_1, total_1, count, covers = refs[11:15]
    surf_2, east_2, south_2, total_2, given_2, total_0 = refs[15:]
    ext, columns = surf.shape
    rows = ext - 2 * HALO
    chunks = columns // LANES
    position = lax.axis_index("gy")
    tail = slice(rows, ext)

    valid, node_row, node_chunk, node_lane = located(far[1:2, :], position, rows, ext, columns)
    key = jnp.where(valid & (node_row >= rows), node_chunk * 8 + (node_row - rows), -1)
    starts, levels = scattered(far[0:1, :], key, node_lane, chunks * 8)
    starting = [
        number[tail, cols(chunk)] + starts[chunk * 8 : chunk * 8 + 8] for chunk in range(chunks)
    ]
    covering = window_sums(starting, corridor, False)
    for chunk in range(chunks):
        at = cols(chunk)
        count[tail, at] = (FEED * DRAIN) * starting[chunk]
        covers[tail, at] = FEED * covering[chunk]
        total_0[tail, at] = FEED * (total[tail, at] + levels[chunk * 8 : chunk * 8 + 8])
    gain = exchange(corridor, tail, surf, total_0, count, covers, total_1)
    for chunk, new_surf in settled(tail, surf, east, south, gain):
        surf_1[tail, cols(chunk)] = new_surf

    every = slice(0, ext)
    gain = exchange(corridor, every, surf_1, total_1, count, covers, total_2)
    fluxes(every, wall_of(ext, tiles), (surf_1, east, south), faces, east_2, south_2)
    for chunk, new_surf in settled(every, surf_1, east_2, south_2, gain):
        surf_2[:, cols(chunk)] = new_surf
    given(corridor, surf_1, given_1, given_2)


def third_kernel(corridor, tiles, surf, east, south, *refs):
    faces = refs[:4]
    total, covers, count, given_2, surf_3, east_3, south_3, total_3, given_3 = refs[4:]
    ext = surf.shape[0]
    own = slice(0, ext - 2 * HALO)
    gain = exchange(corridor, own, surf, total, count, covers, total_3)
    fluxes(own, wall_of(ext, tiles), (surf, east, south), faces, east_3, south_3)
    for chunk, new_surf in settled(own, surf, east_3, south_3, gain):
        surf_3[own, cols(chunk)] = new_surf
    given(corridor, surf, given_2, given_3)


def terms_kernel(corridor, own, surf, given_3, *refs):
    takes, masks, takes_near, masks_near, own_term, partner_term, other_term = refs
    rows, columns = given_3.shape
    owned = own.shape[1]
    chunks = columns // LANES
    levels = [
        given_3[:, cols(chunk)] + DRAIN * surf[:rows, cols(chunk)] for chunk in range(chunks)
    ]
    spare = takes.shape[2] - chunks * rows
    if spare:
        levels.append(jnp.zeros((spare, LANES), jnp.float32))
    levels = jnp.concatenate(levels, axis=0)
    high = levels.astype(jnp.bfloat16)
    low = (levels - high.astype(jnp.float32)).astype(jnp.bfloat16)
    picked = jnp.dot(
        jnp.concatenate([takes[0], takes_near[0], takes[1], takes_near[1]], axis=0),
        jnp.concatenate([high, low], axis=1),
        preferred_element_type=jnp.float32,
    )
    hit = jnp.concatenate([masks[0], masks_near[0], masks[1], masks_near[1]], axis=0)
    picked = (picked * jnp.concatenate([hit, hit], axis=1)).astype(jnp.bfloat16)
    picked = jnp.concatenate([picked[: 3 * owned], picked[3 * owned :]], axis=1)
    terms = lax.dot_general(
        jnp.ones((8, 4 * LANES), jnp.bfloat16),
        picked,
        (((1,), (1,)), ((), ())),
        preferred_element_type=jnp.float32,
    )[0:1]
    own_term[...] = (1.0 - corridor * DRAIN) ** STEPS * own[0:1, :] + terms[:, :owned]
    partner_term[...] = terms[:, owned : 2 * owned]
    other_term[...] = terms[:, 2 * owned :]


def last_kernel(corridor, tiles, surf_2, east_2, south_3, *refs):
    faces = refs[:4]
    total_2, total_3, covers, bed, _, east_3 = refs[4:10]
    surf_3, depth_out, east_out, south_out, depth_4, east_4, south_4, east_tail, sems = refs[10:]
    ext, columns = surf_2.shape
    rows = ext - 2 * HALO
    own, tail = slice(0, rows), slice(rows, ext)
    gain = exchange(corridor, tail, surf_2, total_2, None, covers, None)
    fluxes(tail, None, (surf_2, east_2, None), faces, east_tail)
    for chunk, new_surf in settled(tail, surf_2, east_tail, south_3, gain):
        surf_3[tail, cols(chunk)] = new_surf
    copies = [
        pltpu.make_async_copy(source.at[pl.ds(0, rows), :], target, sems.at[slot])
        for slot, (source, target) in enumerate(
            ((east_4, east_out), (south_4, south_out), (depth_4, depth_out))
        )
    ]
    fluxes(own, wall_of(ext, tiles), (surf_3, east_3, south_3), faces, east_4, south_4)
    copies[0].start()
    copies[1].start()
    gain = exchange(corridor, own, surf_3, total_3, None, covers, None)
    for chunk, new_surf in settled(own, surf_3, east_4, south_4, gain):
        at = cols(chunk)
        depth_4[:, at] = new_surf - bed[own, at]
    copies[2].start()
    for copy in copies:
        copy.wait()


def local(
    depth, flux_east, flux_south, river_section, bed_level, rough_class, manning_table, bank_cell
):
    rows, columns = depth.shape
    owned = river_section.shape[0]
    corridor = bank_cell.shape[0]
    tiles = lax.axis_size("gy")
    ext = rows + 2 * HALO
    chunks = columns // LANES
    partner_section = swapped(river_section, 0).reshape(1, owned)
    partner_cells = swapped(bank_cell, 0)

    def held(value):
        return pltpu.with_memory_space_constraint(value, pltpu.VMEM)

    def far(value):
        return pltpu.with_memory_space_constraint(value, pltpu.HBM)

    params = pltpu.CompilerParams(vmem_limit_bytes=VMEM_LIMIT)
    halo = pltpu.VMEM((5, HALO, columns), jnp.float32)
    field = pltpu.VMEM((ext, columns), jnp.float32)
    small = pltpu.VMEM((rows, columns), jnp.float32)
    term = pltpu.VMEM((1, owned), jnp.float32)
    pair = pltpu.VMEM((2, owned), jnp.float32)
    result = pltpu.HBM((rows, columns), jnp.float32)
    cells = -(-chunks * rows // LANES) * LANES

    def call(kernel, name, outs, values, scratch=(), aliases=None):
        return pl.pallas_call(
            kernel,
            out_shape=outs,
            in_specs=[VMEM_SPEC] * len(values),
            out_specs=[HBM_SPEC if out is result else VMEM_SPEC for out in outs],
            scratch_shapes=scratch,
            input_output_aliases=aliases or {},
            compiler_params=params,
            name=name,
        )(*[held(value) for value in values])

    def picks(nodes):
        return [
            pltpu.VMEM((2, nodes, cells), jnp.bfloat16),
            pltpu.VMEM((2, nodes, LANES), jnp.float32),
        ]

    to_other, own = pl.pallas_call(
        pack_kernel,
        out_shape=[halo, pair],
        in_specs=[HBM_SPEC] * 7,
        out_specs=[VMEM_SPEC] * 2,
        scratch_shapes=[
            pltpu.VMEM((4, 8, columns), jnp.float32),
            pltpu.VMEM((8, columns), jnp.int32),
            pltpu.VMEM((corridor, owned), jnp.int32),
            pltpu.SemaphoreType.DMA((7,)),
        ],
        compiler_params=params,
        name="pack",
    )(
        *[far(value) for value in (depth, bed_level, rough_class, flux_east, flux_south)],
        far(river_section.reshape(1, owned)),
        far(bank_cell),
    )
    (to_other,) = call(
        join_kernel,
        "join",
        [halo],
        (to_other, own, partner_section, partner_cells),
        aliases={0: 0},
    )
    by_other = swapped(to_other, 1)
    classes = manning_table.shape[0]
    to_partner, *loaded, rough, table_rows = pl.pallas_call(
        load_kernel,
        out_shape=[halo]
        + [field] * 4
        + [pltpu.VMEM((rows, columns), jnp.int32), pltpu.VMEM((classes, LANES), jnp.float32)],
        in_specs=[HBM_SPEC] * 6,
        out_specs=[VMEM_SPEC] * 7,
        scratch_shapes=[pltpu.VMEM((1, classes), jnp.float32), pltpu.SemaphoreType.DMA((6,))],
        compiler_params=params,
        name="load",
    )(
        *[far(value) for value in (depth, flux_east, flux_south, bed_level, rough_class)],
        far(manning_table.reshape(1, classes)),
    )
    by_partner = swapped(to_partner, 0)
    *fields, takes, masks = call(
        functools.partial(prepare_kernel, corridor),
        "prepare",
        [field] * 11 + picks(2 * owned),
        (table_rows, rough, own, partner_section, partner_cells, *loaded),
        aliases={5 + slot: slot for slot in range(4)},
    )
    near, beyond = call(relay_kernel, "relay", [pair, pair], (by_other, masks))
    from_far = swapped(near, 0)
    *fields, takes_near, masks_near = call(
        functools.partial(border_kernel, corridor, tiles),
        "border",
        [field] * 11 + picks(owned),
        (by_partner, by_other, table_rows, near, beyond, *fields),
        aliases={5 + slot: slot for slot in range(11)},
    )
    surf, east, south, bed, _, *faces, number, total = fields
    surf_1, total_1, count, covers, given_1 = call(
        functools.partial(first_kernel, corridor),
        "first",
        [field] * 4 + [small],
        (surf, east, south, number, total),
        scratch=[field],
    )
    surf_1, total_1, count, covers, surf_2, east_2, south_2, total_2, given_2 = call(
        functools.partial(second_kernel, corridor, tiles),
        "second",
        [field] * 8 + [small],
        (
            *(from_far, surf, east, south, *faces, number, total, given_1),
            *(surf_1, total_1, count, covers),
        ),
        scratch=[field],
        aliases={11 + slot: slot for slot in range(4)},
    )
    surf_3, east_3, south_3, total_3, given_3 = call(
        functools.partial(third_kernel, corridor, tiles),
        "third",
        [field] * 4 + [small],
        (surf_2, east_2, south_2, *faces, total_2, covers, count, given_2),
    )
    own_term, partner_term, other_term = call(
        functools.partial(terms_kernel, corridor),
        "terms",
        [term] * 3,
        (own, surf_3, given_3, takes, masks, takes_near, masks_near),
    )
    from_other = swapped(other_term.reshape(owned), 1)
    from_partner = swapped(partner_term.reshape(owned), 0)
    _, depth, flux_east, flux_south = call(
        functools.partial(last_kernel, corridor, tiles),
        "last",
        [field, result, result, result],
        (surf_2, east_2, south_3, *faces, total_2, total_3, covers, bed, surf_3, east_3),
        scratch=[small, small, field, field, pltpu.SemaphoreType.DMA((3,))],
        aliases={11: 0},
    )
    river_section = own_term.reshape(owned) + from_other + from_partner
    return (depth, flux_east, flux_south, river_section)


def solution(mesh):
    return jax.shard_map(
        local,
        mesh=mesh,
        in_specs=(
            P(("runs", "gy"), None),
            P(("runs", "gy"), None),
            P(("runs", "gy"), None),
            P(("runs", "gy")),
            P("gy", None),
            P("gy", None),
            P(),
            P(None, "gy"),
        ),
        out_specs=(
            P(("runs", "gy"), None),
            P(("runs", "gy"), None),
            P(("runs", "gy"), None),
            P(("runs", "gy")),
        ),
        check_vma=False,
    )
```

profile of v0, /device:TPU:7, one launch (start us, length us, event | category | flops | bytes accessed | tf_op | source)
XLA Modules:
  0.0 21.0 jit_solution(10432839548667404288)
XLA Ops:
  0.6 0.7 %collective-permute-start.1 = (s32[4,128]{1,0:T(4,128)}, s32[4,128]{1,0:T(4,128)S(1)}, u32[]{:S(2)}, u32[]{:S(2)}) collective-permute-start(s32[4,128]{1,0:T(4,128)} %cells.1), channel_id=1, source_target_pairs={{0,1},{1,0},{2,3},{3,2},{4,5},{5,4},{6,7},{7,6},{8,9},{9,8},{10,11... | collective-permute-start | bytes 6152 | tf_op jit(solution)/shard_map/ppermute | solution.py:37
  1.4 0.1 collective-permute-start
  1.4 1.0 %pack.1 = (f32[5,4,1920]{2,1,0:T(4,128)S(1)}, f32[2,128]{1,0:T(2,128)S(1)}) custom-call(f32[32,1920]{1,0:T(8,128)} %depth_in.1, f32[32,1920]{1,0:T(8,128)} %bed_in.1, s32[32,1920]{1,0:T(8,128)} %rough_in.1, f32[32,1920]{1,0:T(8,128)} %east_in.1, f32[32,1920]{1,0:T(8,128)} %south_in.1, f32[1,128]{1,0:T(1,128)} %bitcast.13, s32[4,128]{1,0:T(4,128)} %cells.1), custom_call_target="tpu_custom_call" | custom-call | tf_op jit(solution)/shard_map/pack/pallas_call | solution.py:633
  2.5 0.2 collective-permute-done
  2.6 0.0 collective-permute-done.1.cells.partner_cells
  2.6 3.4 %collective-permute-start.2 = (f32[5,4,1920]{2,1,0:T(4,128)S(1)}, f32[5,4,1920]{2,1,0:T(4,128)S(1)}, u32[]{:S(2)}, u32[]{:S(2)}) collective-permute-start(f32[5,4,1920]{2,1,0:T(4,128)S(1)} %join.1), channel_id=1, source_target_pairs={{1,2},{2,1},{3,4},{4,3},{5,6},{6,5},{7,8},{8,7},{9,10},{10,9},{11,... | collective-permute-start | bytes 460808 | tf_op jit(solution)/shard_map/ppermute | solution.py:37
  6.0 1.5 %load.1 = (f32[5,4,1920]{2,1,0:T(4,128)S(1)}, f32[40,1920]{1,0:T(8,128)S(1)}, f32[40,1920]{1,0:T(8,128)S(1)}, f32[40,1920]{1,0:T(8,128)S(1)}, f32[40,1920]{1,0:T...) custom-call(f32[32,1920]{1,0:T(8,128)} %depth_in.1, f32[32,1920]{1,0:T(8,128)} %east_in.1, ...), custom_call_target="tpu_custom_call" | custom-call | tf_op jit(solution)/shard_map/load/pallas_call | solution.py:660
  7.5 0.1 collective-permute-start.4
  7.5 1.0 %prepare.1 = (f32[40,1920]{1,0:T(8,128)S(1)}, f32[40,1920]{1,0:T(8,128)S(1)}, f32[40,1920]{1,0:T(8,128)S(1)}, f32[40,1920]{1,0:T(8,128)S(1)}, f32[40,1920]{1,0:T...) custom-call(f32[8,128]{1,0:T(8,128)S(1)} %get-tuple-element.65.table, ...), custom_call_target="tpu_custom_call", output_to_operand_aliasing={{0}: (5, {}), {1}: (6, {}), {2}: (7, {}), {3}: (8, {})} | custom-call | tf_op jit(solution)/shard_map/prepare/pallas_call | solution.py:616
  8.5 1.7 %collective-permute-done.2.by_other = f32[5,4,1920]{2,1,0:T(4,128)S(1)} collective-permute-done((f32[5,4,1920]{2,1,0:T(4,128)S(1)}, f32[5,4,1920]{2,1,0:T(4,128)S(1)}, u32[]{:S(2)}, u32[]{:S(2)}) %collective-permute-start.2) | collective-permute-done | bytes 153632 | tf_op jit(solution)/shard_map/ppermute | solution.py:37
  10.2 1.0 %collective-permute-start.3 = (f32[2,128]{1,0:T(2,128)S(1)}, f32[2,128]{1,0:T(2,128)S(1)}, u32[]{:S(2)}, u32[]{:S(2)}) collective-permute-start(f32[2,128]{1,0:T(2,128)S(1)} %get-tuple-element.72.near), channel_id=1, source_target_pairs={{0,1},{1,0},{2,3},{3,2},{4,5},{5,4},{6,7},{7,6},{8,9},{9,8},{10,11... | collective-permute-start | bytes 3080 | tf_op jit(solution)/shard_map/ppermute | solution.py:37
  11.1 0.0 collective-permute-done.4.by_partner
  11.1 0.6 %border.1 = (f32[40,1920]{1,0:T(8,128)S(1)}, f32[40,1920]{1,0:T(8,128)S(1)}, f32[40,1920]{1,0:T(8,128)S(1)}, f32[40,1920]{1,0:T(8,128)S(1)}, f32[40,1920]{1,0:T(...) custom-call(f32[5,4,1920]{2,1,0:T(4,128)S(1)} %collective-permute-do, ...), custom_call_target="tpu_custom_call", output_to_operand_aliasing={{0}: (5, {}), {1}: (6, {}), {2}: (7, {}), {3}: (8, {}), {4}... | custom-call | tf_op jit(solution)/shard_map/border/pallas_call | solution.py:616
  11.8 0.5 %first.1 = (f32[40,1920]{1,0:T(8,128)S(1)}, f32[40,1920]{1,0:T(8,128)S(1)}, f32[40,1920]{1,0:T(8,128)S(1)}, f32[40,1920]{1,0:T(8,128)S(1)}, f32[32,1920]{1,0:T(8,128)S(1)}) custom-call(f32[40,1920]{1,0:T(8,128)S(1)} %get-tuple-element.86.surf, f32[40,1920]{1,0:T(8,128)S(1)} %get-tuple-element.87.east, f32[40,1920]{1,0:T(8,128)S(1)} %get-tuple-element.88.south, ...), custom_call_target="tpu_custom_call" | custom-call | tf_op jit(solution)/shard_map/first/pallas_call | solution.py:616
  12.2 0.0 collective-permute-done.3.far
  12.2 1.1 %second.1 = (f32[40,1920]{1,0:T(8,128)S(1)}, f32[40,1920]{1,0:T(8,128)S(1)}, f32[40,1920]{1,0:T(8,128)S(1)}, f32[40,1920]{1,0:T(8,128)S(1)}, f32[40,1920]{1,0:T(...) custom-call(f32[2,128]{1,0:T(2,128)S(1)} %collective-permute-done.3., ...), custom_call_target="tpu_custom_call", output_to_operand_aliasing={{0}: (11, {}), {1}: (12, {}), {2}: (13, {}), {3}: (14, {})} | custom-call | tf_op jit(solution)/shard_map/second/pallas_call | solution.py:616
  13.3 0.8 %third.1 = (f32[40,1920]{1,0:T(8,128)S(1)}, f32[40,1920]{1,0:T(8,128)S(1)}, f32[40,1920]{1,0:T(8,128)S(1)}, f32[40,1920]{1,0:T(8,128)S(1)}, f32[32,1920]{1,0:T(8,128)S(1)}) custom-call(f32[40,1920]{1,0:T(8,128)S(1)} %get-tuple-element.100.surf.surf_2, f32[40,1920]{1,0:T(8,128)S(1)} %get-tuple-element.101.east.east_2, ...), custom_call_target="tpu_custom_call" | custom-call | tf_op jit(solution)/shard_map/third/pallas_call | solution.py:616
  14.1 0.6 %terms.1 = (f32[1,128]{1,0:T(1,128)S(1)}, f32[1,128]{1,0:T(1,128)S(1)}, f32[1,128]{1,0:T(1,128)S(1)}) custom-call(f32[2,128]{1,0:T(2,128)S(1)} %get-tuple-element.64.own, f32[40,1920]{1,0:T(8,128)S(1)} %get-tuple-element.110.refs_8_.surf, f32[32,1920]{1,0:T(8,128)S(1)} %get-tuple-element.115.given_3, bf16[2,256,512]{2,1,0:T(8,128)(2,1)S(1)} %get-tuple-element.116.refs_0_, ...), custom_call_target="tpu_custom_call" | custom-call | tf_op jit(solution)/shard_map/terms/pallas_call | solution.py:616
  14.7 3.2 %collective-permute-start.5 = (f32[128]{0:T(128)S(1)}, f32[128]{0:T(128)S(1)}, u32[]{:S(2)}, u32[]{:S(2)}) collective-permute-start(f32[128]{0:T(128)S(1)} %bitcast.12), channel_id=1, source_target_pairs={{1,2},{2,1},{3,4},{4,3},{5,6},{6,5},{7,8},{8,7},{9,10},{10,9},{11,... | collective-permute-start | bytes 1544 | tf_op jit(solution)/shard_map/ppermute | solution.py:37
  17.9 0.1 collective-permute-start.6
  18.0 1.5 %last.1 = (f32[40,1920]{1,0:T(8,128)S(1)}, f32[32,1920]{1,0:T(8,128)}, f32[32,1920]{1,0:T(8,128)}, f32[32,1920]{1,0:T(8,128)}) custom-call(f32[40,1920]{1,0:T(8,128)S(1)} %get-tuple-element.100.surf.surf_2, f32[40,1920]{1,0:T(8,128)S(1)} %get-tuple-element.101.east.east_2, ...), custom_call_target="tpu_custom_call", output_to_operand_aliasing={{0}: (11, {})} | custom-call | tf_op jit(solution)/shard_map/last/pallas_call | solution.py:616
  19.6 0.9 %collective-permute-done.5 = f32[128]{0:T(128)S(1)} collective-permute-done((f32[128]{0:T(128)S(1)}, f32[128]{0:T(128)S(1)}, u32[]{:S(2)}, u32[]{:S(2)}) %collective-permute-start.5) | collective-permute-done | bytes 544 | tf_op jit(solution)/shard_map/ppermute | solution.py:37
  20.5 0.0 collective-permute-done.6
  20.5 0.5 %fusion = f32[128]{0:T(128)} fusion(f32[128]{0:T(128)S(1)} %collective-permute-done.6, f32[128]{0:T(128)S(1)} %collective-permute-done.5, f32[1,128]{1,0:T(1,128)S(1)} %get-tuple-element.119), kind=kLoop, calls=%fused_computation.1 | loop fusion | flops 256 | bytes 2048 | tf_op jit(solution)/shard_map/add | solution.py:732
  (2 shorter events, 0.0 us)
Async XLA Ops:
  0.6 2.0 %collective-permute-start.1 = (s32[4,128]{1,0:T(4,128)}, s32[4,128]{1,0:T(4,128)S(1)}, u32[]{:S(2)}, u32[]{:S(2)}) collective-permute-start(s32[4,128]{1,0:T(4,128)} %cells.1), channel_id=1, source_target_pairs={{0,1},{1,0},{2,3},{3,2},{4,5},{5,4},{6,7},{7,6},{8,9},{9,8},{10,11... | collective-permute-start | bytes 6152 | tf_op jit(solution)/shard_map/ppermute | solution.py:37
  1.4 1.3 %collective-permute-start = (f32[128]{0:T(128)}, f32[128]{0:T(128)S(1)}, u32[]{:S(2)}, u32[]{:S(2)}) collective-permute-start(f32[128]{0:T(128)} %param.11), channel_id=1, source_target_pairs={{0,1},{1,0},{2,3},{3,2},{4,5},{5,4},{6,7},{7,6},{8,9},{9,8},{10,11... | collective-permute-start | bytes 1544 | tf_op jit(solution)/shard_map/ppermute | solution.py:37
  2.6 7.5 %collective-permute-start.2 = (f32[5,4,1920]{2,1,0:T(4,128)S(1)}, f32[5,4,1920]{2,1,0:T(4,128)S(1)}, u32[]{:S(2)}, u32[]{:S(2)}) collective-permute-start(f32[5,4,1920]{2,1,0:T(4,128)S(1)} %join.1), channel_id=1, source_target_pairs={{1,2},{2,1},{3,4},{4,3},{5,6},{6,5},{7,8},{8,7},{9,10},{10,9},{11,... | collective-permute-start | bytes 460808 | tf_op jit(solution)/shard_map/ppermute | solution.py:37
  7.5 3.7 %collective-permute-start.4 = (f32[5,4,1920]{2,1,0:T(4,128)S(1)}, f32[5,4,1920]{2,1,0:T(4,128)S(1)}, u32[]{:S(2)}, u32[]{:S(2)}) collective-permute-start(f32[5,4,1920]{2,1,0:T(4,128)S(1)} %get-tuple-element.73), channel_id=1, source_target_pairs={{0,1},{1,0},{2,3},{3,2},{4,5},{5,4},{6,7},{7,6},{8,9},{9,8},{10,11... | collective-permute-start | bytes 460808 | tf_op jit(solution)/shard_map/ppermute | solution.py:37
  10.2 2.0 %collective-permute-start.3 = (f32[2,128]{1,0:T(2,128)S(1)}, f32[2,128]{1,0:T(2,128)S(1)}, u32[]{:S(2)}, u32[]{:S(2)}) collective-permute-start(f32[2,128]{1,0:T(2,128)S(1)} %get-tuple-element.72.near), channel_id=1, source_target_pairs={{0,1},{1,0},{2,3},{3,2},{4,5},{5,4},{6,7},{7,6},{8,9},{9,8},{10,11... | collective-permute-start | bytes 3080 | tf_op jit(solution)/shard_map/ppermute | solution.py:37
  14.7 5.8 %collective-permute-start.5 = (f32[128]{0:T(128)S(1)}, f32[128]{0:T(128)S(1)}, u32[]{:S(2)}, u32[]{:S(2)}) collective-permute-start(f32[128]{0:T(128)S(1)} %bitcast.12), channel_id=1, source_target_pairs={{1,2},{2,1},{3,4},{4,3},{5,6},{6,5},{7,8},{8,7},{9,10},{10,9},{11,... | collective-permute-start | bytes 1544 | tf_op jit(solution)/shard_map/ppermute | solution.py:37
  17.9 2.5 %collective-permute-start.6 = (f32[128]{0:T(128)S(1)}, f32[128]{0:T(128)S(1)}, u32[]{:S(2)}, u32[]{:S(2)}) collective-permute-start(f32[128]{0:T(128)S(1)} %bitcast.11), channel_id=1, source_target_pairs={{0,1},{1,0},{2,3},{3,2},{4,5},{5,4},{6,7},{7,6},{8,9},{9,8},{10,11... | collective-permute-start | bytes 1544 | tf_op jit(solution)/shard_map/ppermute | solution.py:37
where the time goes:
time: 21.4 us; the launch traced here: 21 us
  starting transfers between devices  8.51 us (40%)
  Pallas kernels  8.47 us (40%)
  waiting for transfers between devices  2.75 us (13%)
  between operations  0.74 us (3%)
  other arithmetic  0.52 us (2%)
    ppermute x7, starting transfers between devices, swapped(): return lax.ppermute(value, 'gy', pairs)  8.51 us
    pallas_call x9, Pallas kernels, call(): pl.pallas_call(kernel, out_shape=outs, in_specs=[VMEM_SPEC] * len(values)...  6 us
    ppermute x7, waiting for transfers between devices, swapped(): return lax.ppermute(value, 'gy', pairs)  2.75 us
    pallas_call x1, Pallas kernels, local(): pl.pallas_call(load_kernel, out_shape=[halo] + [field] * 4 + [pltpu.VMEM(...  1.45 us
    pallas_call x1, Pallas kernels, local(): pl.pallas_call(pack_kernel, out_shape=[halo, pair], in_specs=[HBM_SPEC] *...  1.02 us
    add x1, other arithmetic, local(): river_section = own_term.reshape(owned) + from_other + from_partner  0.52 us
  transfers between devices with their start and end apart: 7, of which 3 were waited for; matrix products, arithmetic and copies ran while one was open for 0% of the time, Pallas kernels for 29%

commit v1 on v0

--- a/solution.py
+++ b/solution.py
@@ -153,55 +153,93 @@
     return number, total
 
 
+def border_rows(first, last, put):
+    row = lax.broadcasted_iota(jnp.int32, (HALO, LANES), 0)
+
+    def low(fields, south):
+        for slot, value in enumerate(fields):
+            put(slot, jnp.where(row == HALO - 1, south[slot : slot + 1], value[:HALO]))
+
+    def high(fields, south):
+        for slot, value in enumerate(fields):
+            flux = south[HALO + slot : HALO + slot + 1]
+            put(slot, jnp.where(row == 0, flux, value[HALO:]))
+
+    if first is not None:
+        low(*first)
+    if last is not None:
+        high(*last)
+
+
 def pack_kernel(
-    depth, bed, rough, east, south, section, cells, to_other, own, held, held_rough, held_cells, sems
+    depth, bed, rough, east, south, section, cells, table_in, to_other, own, *refs
 ):
+    held, held_rough, held_cells, table, sems = refs
     rows, columns = depth.shape
+    chunks = columns // LANES
     even = lax.axis_index("gy") % 2 == 0
     start = pl.multiple_of(jnp.where(even, 0, rows - 8), 8)
+    near = pl.ds(start, 8)
     copies = [
         pltpu.make_async_copy(source, target, sems.at[slot])
         for slot, (source, target) in enumerate(
             (
-                (depth.at[pl.ds(start, 8), :], held.at[0]),
-                (bed.at[pl.ds(start, 8), :], held.at[1]),
-                (rough.at[pl.ds(start, 8), :], held_rough),
-                (east.at[pl.ds(start, 8), :], held.at[2]),
-                (south.at[pl.ds(start, 8), :], held.at[3]),
+                (rough.at[near, :], held_rough),
+                (bed.at[near, :], held.at[1]),
+                (depth.at[near, :], held.at[0]),
+                (east.at[near, :], held.at[2]),
+                (south.at[near, :], held.at[3]),
                 (section, own.at[pl.ds(0, 1), :]),
                 (cells, held_cells),
+                (table_in, table),
             )
         )
     ]
     for copy in copies:
         copy.start()
-    for slot in range(5):
-        copies[slot].wait()
-        block = (
-            held_rough[...].astype(jnp.float32) if slot == 2 else held[slot - (slot > 2)]
-        )
-        to_other[slot] = jnp.where(even, block[:HALO], block[8 - HALO :])
-    for copy in copies[5:]:
+    for copy in copies:
         copy.wait()
     own[1:2, :] = (held_cells[0:1, :] + 1).astype(jnp.float32)
-
-
-def join_kernel(before, own, section, cells, to_other):
-    even = lax.axis_index("gy") % 2 == 0
-    owned = own.shape[1]
-    rows = (own[0:1, :], own[1:2, :], section[...], (cells[0:1, :] + 1).astype(jnp.float32))
-
-    def put(spare):
-        for slot, row in enumerate(rows):
-            to_other[3, spare : spare + 1, slot * owned : (slot + 1) * owned] = row
-
-    @pl.when(even)
-    def _():
-        put(HALO - 1)
-
-    @pl.when(jnp.logical_not(even))
-    def _():
-        put(0)
+    entries = [
+        jnp.broadcast_to(table[:, k : k + 1], (1, LANES)) for k in range(table.shape[1])
+    ]
+    manns = [looked_up(held_rough[:, cols(chunk)], entries) for chunk in range(chunks)]
+    row = lax.broadcasted_iota(jnp.int32, (8, LANES), 0)
+    for chunk in range(chunks):
+        at, then = cols(chunk), cols(min(chunk + 1, chunks - 1))
+        m0, b0 = manns[chunk], held[1, :, at]
+        s0 = held[0, :, at] + b0
+        m1, b1 = manns[min(chunk + 1, chunks - 1)], held[1, :, then]
+        s1 = held[0, :, then] + b1
+        bed_max = jnp.maximum(b0, moved_left(b0, b1, 1))
+        drag = drag_of(m0, moved_left(m0, m1, 1))
+        new_east = face(held[2, :, at], s0, moved_left(s0, s1, 1), bed_max, drag)
+        new_east = east_walled(new_east, chunk, chunks)
+        bed_max = jnp.maximum(b0, moved_up(b0))
+        drag = drag_of(m0, moved_up(m0))
+        q0 = held[3, :, at]
+        new_south = jnp.where(row == 7, q0, face(q0, s0, moved_up(s0), bed_max, drag))
+        fields = (s0, b0, held_rough[:, at].astype(jnp.float32), new_east)
+        lower, upper = {}, {}
+        border_rows((fields, new_south), None, lower.__setitem__)
+        border_rows(None, (fields, new_south), upper.__setitem__)
+        for slot in range(4):
+            to_other[slot, :, at] = jnp.where(even, lower[slot], upper[slot])
+    for slot in range(1, 4):
+        to_other[slot, :, columns:] = jnp.zeros((HALO, LANES), jnp.float32)
+    to_other[0, 0:2, columns:] = own[...]
+
+
+def join_kernel(before, section, cells, to_other):
+    columns = to_other.shape[2] - LANES
+    to_other[0, 2:3, columns:] = section[...]
+    to_other[0, 3:4, columns:] = (cells[0:1, :] + 1).astype(jnp.float32)
+
+
+def relay_kernel(by_other, prepared, near):
+    del prepared
+    columns = by_other.shape[2] - LANES
+    near[...] = by_other[0, 0:2, columns:]
 
 
 def picking(reach, rows, key, lane, takes, masks):
@@ -227,9 +265,8 @@
 def load_kernel(
     depth_in, east_in, south_in, bed_in, rough_in, table_in, *refs
 ):
-    to_partner, surf, east, south, bed, rough, table_rows, table, sems = refs
+    surf, east, south, bed, rough, table_rows, table, sems = refs
     rows, columns = depth_in.shape
-    even = lax.axis_index("gy") % 2 == 0
     own = pl.ds(0, rows)
     copies = [
         pltpu.make_async_copy(source, target.at[own, :], sems.at[slot])
@@ -249,30 +286,13 @@
     copies[5].wait()
     for k in range(table_rows.shape[0]):
         table_rows[k : k + 1, :] = jnp.broadcast_to(table[:, k : k + 1], (1, LANES))
-    for slot, source in enumerate((surf, bed, rough, east, south)):
-        copies[slot].wait()
-        for chunk in range(columns // LANES):
-            at = cols(chunk)
-            first = source[:8, at].astype(jnp.float32)
-            last = source[rows - 8 : rows, at].astype(jnp.float32)
-            to_partner[slot, :, at] = jnp.where(even, last[8 - HALO :], first[:HALO])
-
-
-def relay_kernel(by_other, prepared, near, beyond):
-    del prepared
-    even = lax.axis_index("gy") % 2 == 0
-    owned = near.shape[1]
-    for target, first in ((near, 0), (beyond, 2)):
-        for slot in range(2):
-            mine = slice((first + slot) * owned, (first + slot + 1) * owned)
-            target[slot : slot + 1, :] = jnp.where(
-                even, by_other[3, 0:1, mine], by_other[3, HALO - 1 : HALO, mine]
-            )
+    for copy in copies[:5]:
+        copy.wait()
 
 
 def prepare_kernel(reach, table_rows, rough, own, partner_section, partner_cells, *refs):
     surf, east, south, bed = refs[4:8]
-    mann, bed_e, bed_s, drag_e, drag_s, number, total, takes, masks = refs[8:]
+    mann, bed_e, bed_s, drag_e, drag_s, number, total, takes, masks, to_partner = refs[8:]
     ext, columns = surf.shape
     rows = ext - 2 * HALO
     chunks = columns // LANES
@@ -318,6 +338,20 @@
         q0 = south[:rows, at]
         south[:rows, at] = jnp.where(kept, q0, face(q0, s0, moved_up(s0), bed_max, drag))
 
+    even = position % 2 == 0
+    for chunk in range(chunks):
+        at = cols(chunk)
+
+        def tile(part):
+            fields = (surf[part, at], bed[part, at], rough[part, at].astype(jnp.float32))
+            return (*fields, east[part, at]), south[part, at]
+
+        lower, upper = {}, {}
+        border_rows(tile(slice(0, 8)), None, lower.__setitem__)
+        border_rows(None, tile(slice(rows - 8, rows)), upper.__setitem__)
+        for slot in range(4):
+            to_partner[slot, :, at] = jnp.where(even, upper[slot], lower[slot])
+
 
 def wall_of(ext, tiles):
     position = lax.axis_index("gy")
@@ -326,7 +360,7 @@
     return ((row == ext - 1) & (position == 0)) | ((row == rows - 1) & (position == tiles - 1))
 
 
-def border_kernel(reach, tiles, by_partner, by_other, table_rows, near, beyond, *refs):
+def border_kernel(reach, tiles, by_partner, by_other, table_rows, near, *refs):
     surf, east, south, bed, mann, bed_e, bed_s, drag_e, drag_s, number, total, takes, masks = refs[11:]
     ext, columns = surf.shape
     rows = ext - 2 * HALO
@@ -335,21 +369,24 @@
     even = position % 2 == 0
     entries = [table_rows[k : k + 1, :] for k in range(table_rows.shape[0])]
     row = lax.broadcasted_iota(jnp.int32, (2 * HALO, LANES), 0)
-    spare = jnp.where(even, HALO, HALO - 1)
     for chunk in range(chunks):
         at = cols(chunk)
         halos = []
-        for slot in range(5):
+        flux = jnp.zeros((2 * HALO, LANES), jnp.float32)
+        for slot in range(4):
             a, b = by_partner[slot, :, at], by_other[slot, :, at]
             below = jnp.where(even, a, b)
             above = jnp.where(even, b, a)
             halos.append(jnp.concatenate([below, above], axis=0))
-        surf[rows:, at] = halos[0] + halos[1]
+            flux = jnp.where(row == slot, below[HALO - 1 :], flux)
+            flux = jnp.where(row == HALO + slot, above[:1], flux)
+        surf[rows:, at] = halos[0]
         bed[rows:, at] = halos[1]
         mann[rows:, at] = looked_up(halos[2].astype(jnp.int32), entries)
-        east[rows:, at] = jnp.where(row == spare, 0.0, halos[3])
-        south[rows:, at] = halos[4]
-
+        east[rows:, at] = halos[3]
+        south[rows:, at] = flux
+
+    beyond = by_other[0, 2:4, columns:]
     section = jnp.concatenate([near[0:1, :], beyond[0:1, :]], axis=1)
     cell = jnp.concatenate([near[1:2, :], beyond[1:2, :]], axis=1)
     valid, node_row, node_chunk, node_lane = located(cell, position, rows, ext, columns)
@@ -361,20 +398,14 @@
     picking(reach, rows, key[:, :owned], node_lane[:, :owned], takes, masks)
 
     wall = wall_of(ext, tiles)
-    kept = lax.broadcasted_iota(jnp.int32, (16, LANES), 0) < 7
+    kept = lax.broadcasted_iota(jnp.int32, (16, LANES), 0) % 8 < 7
     for chunk in range(chunks):
         at, then = cols(chunk), cols(min(chunk + 1, chunks - 1))
         number[:, at] += starts[chunk * ext : (chunk + 1) * ext]
         total[:, at] += levels[chunk * ext : (chunk + 1) * ext]
-        s0, b0, m0 = surf[rows:, at], bed[rows:, at], mann[rows:, at]
-        bed_max = jnp.maximum(b0, moved_left(b0, bed[rows:, then], 1))
-        drag = drag_of(m0, moved_left(m0, mann[rows:, then], 1))
-        bed_e[rows:, at] = bed_max
-        drag_e[rows:, at] = drag
-        new_east = face(
-            east[rows:, at], s0, moved_left(s0, surf[rows:, then], 1), bed_max, drag
-        )
-        east[rows:, at] = east_walled(new_east, chunk, chunks)
+        b0, m0 = bed[rows:, at], mann[rows:, at]
+        bed_e[rows:, at] = jnp.maximum(b0, moved_left(b0, bed[rows:, then], 1))
+        drag_e[rows:, at] = drag_of(m0, moved_left(m0, mann[rows:, then], 1))
 
         def rolled_up(ref):
             value = jnp.concatenate([ref[rows - 8 :, at], ref[:8, at]], axis=0)
@@ -388,8 +419,8 @@
         bed_s[rows - 8 :, at] = bed_max
         drag_s[rows - 8 :, at] = drag
         q0 = south[rows - 8 :, at]
-        new_south = jnp.where(wall, 0.0, face(q0, s0, s1, bed_max, drag))
-        south[rows - 8 :, at] = jnp.where(kept, q0, new_south)
+        new_south = jnp.where(kept, q0, face(q0, s0, s1, bed_max, drag))
+        south[rows - 8 :, at] = jnp.where(wall, 0.0, new_south)
 
 
 def fluxes(mine, wall, before, faces, east_out, south_out=None):
@@ -604,7 +635,8 @@
         return pltpu.with_memory_space_constraint(value, pltpu.HBM)
 
     params = pltpu.CompilerParams(vmem_limit_bytes=VMEM_LIMIT)
-    halo = pltpu.VMEM((5, HALO, columns), jnp.float32)
+    halo = pltpu.VMEM((4, HALO, columns), jnp.float32)
+    wide = pltpu.VMEM((4, HALO, columns + LANES), jnp.float32)
     field = pltpu.VMEM((ext, columns), jnp.float32)
     small = pltpu.VMEM((rows, columns), jnp.float32)
     term = pltpu.VMEM((1, owned), jnp.float32)
@@ -630,16 +662,20 @@
             pltpu.VMEM((2, nodes, LANES), jnp.float32),
         ]
 
+    classes = manning_table.shape[0]
+    table = far(manning_table.reshape(1, classes))
+    table_held = pltpu.VMEM((1, classes), jnp.float32)
     to_other, own = pl.pallas_call(
         pack_kernel,
-        out_shape=[halo, pair],
-        in_specs=[HBM_SPEC] * 7,
+        out_shape=[wide, pair],
+        in_specs=[HBM_SPEC] * 8,
         out_specs=[VMEM_SPEC] * 2,
         scratch_shapes=[
             pltpu.VMEM((4, 8, columns), jnp.float32),
             pltpu.VMEM((8, columns), jnp.int32),
             pltpu.VMEM((corridor, owned), jnp.int32),
-            pltpu.SemaphoreType.DMA((7,)),
+            table_held,
+            pltpu.SemaphoreType.DMA((8,)),
         ],
         compiler_params=params,
         name="pack",
@@ -647,46 +683,45 @@
         *[far(value) for value in (depth, bed_level, rough_class, flux_east, flux_south)],
         far(river_section.reshape(1, owned)),
         far(bank_cell),
+        table,
     )
     (to_other,) = call(
         join_kernel,
         "join",
-        [halo],
-        (to_other, own, partner_section, partner_cells),
+        [wide],
+        (to_other, partner_section, partner_cells),
         aliases={0: 0},
     )
     by_other = swapped(to_other, 1)
-    classes = manning_table.shape[0]
-    to_partner, *loaded, rough, table_rows = pl.pallas_call(
+    *loaded, rough, table_rows = pl.pallas_call(
         load_kernel,
-        out_shape=[halo]
-        + [field] * 4
+        out_shape=[field] * 4
         + [pltpu.VMEM((rows, columns), jnp.int32), pltpu.VMEM((classes, LANES), jnp.float32)],
         in_specs=[HBM_SPEC] * 6,
-        out_specs=[VMEM_SPEC] * 7,
-        scratch_shapes=[pltpu.VMEM((1, classes), jnp.float32), pltpu.SemaphoreType.DMA((6,))],
+        out_specs=[VMEM_SPEC] * 6,
+        scratch_shapes=[table_held, pltpu.SemaphoreType.DMA((6,))],
         compiler_params=params,
         name="load",
     )(
         *[far(value) for value in (depth, flux_east, flux_south, bed_level, rough_class)],
-        far(manning_table.reshape(1, classes)),
-    )
-    by_partner = swapped(to_partner, 0)
-    *fields, takes, masks = call(
+        table,
+    )
+    *fields, takes, masks, to_partner = call(
         functools.partial(prepare_kernel, corridor),
         "prepare",
-        [field] * 11 + picks(2 * owned),
+        [field] * 11 + picks(2 * owned) + [halo],
         (table_rows, rough, own, partner_section, partner_cells, *loaded),
         aliases={5 + slot: slot for slot in range(4)},
     )
-    near, beyond = call(relay_kernel, "relay", [pair, pair], (by_other, masks))
+    by_partner = swapped(to_partner, 0)
+    (near,) = call(relay_kernel, "relay", [pair], (by_other, masks))
     from_far = swapped(near, 0)
     *fields, takes_near, masks_near = call(
         functools.partial(border_kernel, corridor, tiles),
         "border",
         [field] * 11 + picks(owned),
-        (by_partner, by_other, table_rows, near, beyond, *fields),
-        aliases={5 + slot: slot for slot in range(11)},
+        (by_partner, by_other, table_rows, near, *fields),
+        aliases={4 + slot: slot for slot in range(11)},
     )
     surf, east, south, bed, _, *faces, number, total = fields
     surf_1, total_1, count, covers, given_1 = call(

time: 21.4 us -> 21.1 us (0.986)
  the two profiles are of different devices: /device:TPU:7 before, /device:TPU:0 now
where the time goes in v1:
time: 21.1 us; the launch traced here: 20.9 us
  starting transfers between devices  10 us (47%)
  Pallas kernels  8.75 us (41%)
  waiting for transfers between devices  0.89 us (4%)
  between operations  0.76 us (4%)
  other arithmetic  0.52 us (2%)
    ppermute x7, starting transfers between devices, swapped(): return lax.ppermute(value, 'gy', pairs)  10 us
    pallas_call x9, Pallas kernels, call(): pl.pallas_call(kernel, out_shape=outs, in_specs=[VMEM_SPEC] * len(values)...  6.04 us
    pallas_call x1, Pallas kernels, local(): pl.pallas_call(load_kernel, out_shape=[field] * 4 + [pltpu.VMEM((rows, co...  1.44 us
    pallas_call x1, Pallas kernels, local(): pl.pallas_call(pack_kernel, out_shape=[wide, pair], in_specs=[HBM_SPEC] *...  1.27 us
    ppermute x7, waiting for transfers between devices, swapped(): return lax.ppermute(value, 'gy', pairs)  0.89 us
    add x1, other arithmetic, local(): river_section = own_term.reshape(owned) + from_other + from_partner  0.52 us
  transfers between devices with their start and end apart: 7, of which 1 were waited for; matrix products, arithmetic and copies ran while one was open for 0% of the time, Pallas kernels for 30%

profile of v1, /device:TPU:0, one launch (start us, length us, event | category | flops | bytes accessed | tf_op | source)
XLA Modules:
  0.0 20.9 jit_solution(110509762191548821)
XLA Ops:
  0.6 0.5 %collective-permute-start.1 = (s32[4,128]{1,0:T(4,128)}, s32[4,128]{1,0:T(4,128)S(1)}, u32[]{:S(2)}, u32[]{:S(2)}) collective-permute-start(s32[4,128]{1,0:T(4,128)} %cells.1), channel_id=1, source_target_pairs={{0,1},{1,0},{2,3},{3,2},{4,5},{5,4},{6,7},{7,6},{8,9},{9,8},{10,11... | collective-permute-start | bytes 6152 | tf_op jit(solution)/shard_map/ppermute | solution.py:37
  1.1 0.1 collective-permute-start
  1.2 1.3 %pack.1 = (f32[4,4,2048]{2,1,0:T(4,128)S(1)}, f32[2,128]{1,0:T(2,128)S(1)}) custom-call(f32[32,1920]{1,0:T(8,128)} %depth_in.1, f32[32,1920]{1,0:T(8,128)} %bed_in.1, s32[32,1920]{1,0:T(8,128)} %rough_in.1, f32[32,1920]{1,0:T(8,128)} %east_in.1, f32[32,1920]{1,0:T(8,128)} %south_in.1, f32[1,128]{1,0:T(1,128)} %bitcast.15, s32[4,128]{1,0:T(4,128)} %cells.1, ...), custom_call_target="tpu_custom_call" | custom-call | tf_op jit(solution)/shard_map/pack/pallas_call | solution.py:668
  2.5 0.0 collective-permute-done
  2.5 0.0 collective-permute-done.1.cells.partner_cells
  2.5 0.7 %collective-permute-start.2 = (f32[4,4,2048]{2,1,0:T(4,128)S(1)}, f32[4,4,2048]{2,1,0:T(4,128)S(1)}, u32[]{:S(2)}, u32[]{:S(2)}) collective-permute-start(f32[4,4,2048]{2,1,0:T(4,128)S(1)} %join.1), channel_id=1, source_target_pairs={{1,2},{2,1},{3,4},{4,3},{5,6},{6,5},{7,8},{8,7},{9,10},{10,9},{11,... | collective-permute-start | bytes 393224 | tf_op jit(solution)/shard_map/ppermute | solution.py:37
  3.2 1.4 %load.1 = (f32[40,1920]{1,0:T(8,128)S(1)}, f32[40,1920]{1,0:T(8,128)S(1)}, f32[40,1920]{1,0:T(8,128)S(1)}, f32[40,1920]{1,0:T(8,128)S(1)}, s32[32,1920]{1,0:T(8,128)S(1)}, /*index=5*/f32[8,128]{1,0:T(8,128)S(1)}) custom-call(f32[32,1920]{1,0:T(8,128)} %depth_in.1, f32[32,1920]{1,0:T(8,128)} %east_in.1, f32[32,1920]{1,0:T(8,128)} %south_in.1, ...), custom_call_target="tpu_custom_call" | custom-call | tf_op jit(solution)/shard_map/load/pallas_call | solution.py:696
  4.7 1.0 %prepare.1 = (f32[40,1920]{1,0:T(8,128)S(1)}, f32[40,1920]{1,0:T(8,128)S(1)}, f32[40,1920]{1,0:T(8,128)S(1)}, f32[40,1920]{1,0:T(8,128)S(1)}, f32[40,1920]{1,0:T...) custom-call(f32[8,128]{1,0:T(8,128)S(1)} %get-tuple-element.62.table, ...), custom_call_target="tpu_custom_call", output_to_operand_aliasing={{0}: (5, {}), {1}: (6, {}), {2}: (7, {}), {3}: (8, {})} | custom-call | tf_op jit(solution)/shard_map/prepare/pallas_call | solution.py:648
  5.7 4.4 %collective-permute-start.4 = (f32[4,4,1920]{2,1,0:T(4,128)S(1)}, f32[4,4,1920]{2,1,0:T(4,128)S(1)}, u32[]{:S(2)}, u32[]{:S(2)}) collective-permute-start(f32[4,4,1920]{2,1,0:T(4,128)S(1)} %get-tuple-element.70), channel_id=1, source_target_pairs={{0,1},{1,0},{2,3},{3,2},{4,5},{5,4},{6,7},{7,6},{8,9},{9,8},{10,11... | collective-permute-start | bytes 368648 | tf_op jit(solution)/shard_map/ppermute | solution.py:37
  10.1 0.0 collective-permute-done.2.by_other
  10.1 0.1 collective-permute-start.3
  10.2 0.9 %collective-permute-done.4.by_partner = f32[4,4,1920]{2,1,0:T(4,128)S(1)} collective-permute-done((f32[4,4,1920]{2,1,0:T(4,128)S(1)}, f32[4,4,1920]{2,1,0:T(4,128)S(1)}, u32[]{:S(2)}, u32[]{:S(2)}) %collective-permute-start.4) | collective-permute-done | bytes 122912 | tf_op jit(solution)/shard_map/ppermute | solution.py:37
  11.1 0.6 %border.1 = (f32[40,1920]{1,0:T(8,128)S(1)}, f32[40,1920]{1,0:T(8,128)S(1)}, f32[40,1920]{1,0:T(8,128)S(1)}, f32[40,1920]{1,0:T(8,128)S(1)}, f32[40,1920]{1,0:T(...) custom-call(f32[4,4,1920]{2,1,0:T(4,128)S(1)} %collective-permute-do, ...), custom_call_target="tpu_custom_call", output_to_operand_aliasing={{0}: (4, {}), {1}: (5, {}), {2}: (6, {}), {3}: (7, {}), {4}... | custom-call | tf_op jit(solution)/shard_map/border/pallas_call | solution.py:648
  11.7 0.5 %first.1 = (f32[40,1920]{1,0:T(8,128)S(1)}, f32[40,1920]{1,0:T(8,128)S(1)}, f32[40,1920]{1,0:T(8,128)S(1)}, f32[40,1920]{1,0:T(8,128)S(1)}, f32[32,1920]{1,0:T(8,128)S(1)}) custom-call(f32[40,1920]{1,0:T(8,128)S(1)} %get-tuple-element.82.surf, f32[40,1920]{1,0:T(8,128)S(1)} %get-tuple-element.83.east, f32[40,1920]{1,0:T(8,128)S(1)} %get-tuple-element.84.south, ...), custom_call_target="tpu_custom_call" | custom-call | tf_op jit(solution)/shard_map/first/pallas_call | solution.py:648
  12.1 0.0 collective-permute-done.3.far
  12.1 1.1 %second.1 = (f32[40,1920]{1,0:T(8,128)S(1)}, f32[40,1920]{1,0:T(8,128)S(1)}, f32[40,1920]{1,0:T(8,128)S(1)}, f32[40,1920]{1,0:T(8,128)S(1)}, f32[40,1920]{1,0:T(...) custom-call(f32[2,128]{1,0:T(2,128)S(1)} %collective-permute-done.3., ...), custom_call_target="tpu_custom_call", output_to_operand_aliasing={{0}: (11, {}), {1}: (12, {}), {2}: (13, {}), {3}: (14, {})} | custom-call | tf_op jit(solution)/shard_map/second/pallas_call | solution.py:648
  13.2 0.8 %third.1 = (f32[40,1920]{1,0:T(8,128)S(1)}, f32[40,1920]{1,0:T(8,128)S(1)}, f32[40,1920]{1,0:T(8,128)S(1)}, f32[40,1920]{1,0:T(8,128)S(1)}, f32[32,1920]{1,0:T(8,128)S(1)}) custom-call(f32[40,1920]{1,0:T(8,128)S(1)} %get-tuple-element.96.surf.surf_2, f32[40,1920]{1,0:T(8,128)S(1)} %get-tuple-element.97.east.east_2, f32[40,1920]{1,0:T(8,128)S(1)} %get-tuple-element.98.south, ...), custom_call_target="tpu_custom_call" | custom-call | tf_op jit(solution)/shard_map/third/pallas_call | solution.py:648
  14.0 0.6 %terms.1 = (f32[1,128]{1,0:T(1,128)S(1)}, f32[1,128]{1,0:T(1,128)S(1)}, f32[1,128]{1,0:T(1,128)S(1)}) custom-call(f32[2,128]{1,0:T(2,128)S(1)} %get-tuple-element.64.own, f32[40,1920]{1,0:T(8,128)S(1)} %get-tuple-element.106.refs_8_.surf, f32[32,1920]{1,0:T(8,128)S(1)} %get-tuple-element.111.given_3, bf16[2,256,512]{2,1,0:T(8,128)(2,1)S(1)} %get-tuple-element.112.refs_0_, ...), custom_call_target="tpu_custom_call" | custom-call | tf_op jit(solution)/shard_map/terms/pallas_call | solution.py:648
  14.6 0.7 %collective-permute-start.5 = (f32[128]{0:T(128)S(1)}, f32[128]{0:T(128)S(1)}, u32[]{:S(2)}, u32[]{:S(2)}) collective-permute-start(f32[128]{0:T(128)S(1)} %bitcast.12), channel_id=1, source_target_pairs={{1,2},{2,1},{3,4},{4,3},{5,6},{6,5},{7,8},{8,7},{9,10},{10,9},{11,... | collective-permute-start | bytes 1544 | tf_op jit(solution)/shard_map/ppermute | solution.py:37
  15.3 3.6 %collective-permute-start.6 = (f32[128]{0:T(128)S(1)}, f32[128]{0:T(128)S(1)}, u32[]{:S(2)}, u32[]{:S(2)}) collective-permute-start(f32[128]{0:T(128)S(1)} %bitcast.11), channel_id=1, source_target_pairs={{0,1},{1,0},{2,3},{3,2},{4,5},{5,4},{6,7},{7,6},{8,9},{9,8},{10,11... | collective-permute-start | bytes 1544 | tf_op jit(solution)/shard_map/ppermute | solution.py:37
  18.9 1.5 %last.1 = (f32[40,1920]{1,0:T(8,128)S(1)}, f32[32,1920]{1,0:T(8,128)}, f32[32,1920]{1,0:T(8,128)}, f32[32,1920]{1,0:T(8,128)}) custom-call(f32[40,1920]{1,0:T(8,128)S(1)} %get-tuple-element.96.surf.surf_2, f32[40,1920]{1,0:T(8,128)S(1)} %get-tuple-element.97.east.east_2, ...), custom_call_target="tpu_custom_call", output_to_operand_aliasing={{0}: (11, {})} | custom-call | tf_op jit(solution)/shard_map/last/pallas_call | solution.py:648
  20.4 0.0 collective-permute-done.5
  20.4 0.0 collective-permute-done.6
  20.4 0.5 %fusion = f32[128]{0:T(128)} fusion(f32[128]{0:T(128)S(1)} %collective-permute-done.6, f32[128]{0:T(128)S(1)} %collective-permute-done.5, f32[1,128]{1,0:T(1,128)S(1)} %get-tuple-element.115), kind=kLoop, calls=%fused_computation.1 | loop fusion | flops 256 | bytes 2048 | tf_op jit(solution)/shard_map/add | solution.py:767
  (2 shorter events, 0.0 us)
Async XLA Ops:
  0.6 1.9 %collective-permute-start.1 = (s32[4,128]{1,0:T(4,128)}, s32[4,128]{1,0:T(4,128)S(1)}, u32[]{:S(2)}, u32[]{:S(2)}) collective-permute-start(s32[4,128]{1,0:T(4,128)} %cells.1), channel_id=1, source_target_pairs={{0,1},{1,0},{2,3},{3,2},{4,5},{5,4},{6,7},{7,6},{8,9},{9,8},{10,11... | collective-permute-start | bytes 6152 | tf_op jit(solution)/shard_map/ppermute | solution.py:37
  1.1 1.4 %collective-permute-start = (f32[128]{0:T(128)}, f32[128]{0:T(128)S(1)}, u32[]{:S(2)}, u32[]{:S(2)}) collective-permute-start(f32[128]{0:T(128)} %param.11), channel_id=1, source_target_pairs={{0,1},{1,0},{2,3},{3,2},{4,5},{5,4},{6,7},{7,6},{8,9},{9,8},{10,11... | collective-permute-start | bytes 1544 | tf_op jit(solution)/shard_map/ppermute | solution.py:37
  2.5 7.6 %collective-permute-start.2 = (f32[4,4,2048]{2,1,0:T(4,128)S(1)}, f32[4,4,2048]{2,1,0:T(4,128)S(1)}, u32[]{:S(2)}, u32[]{:S(2)}) collective-permute-start(f32[4,4,2048]{2,1,0:T(4,128)S(1)} %join.1), channel_id=1, source_target_pairs={{1,2},{2,1},{3,4},{4,3},{5,6},{6,5},{7,8},{8,7},{9,10},{10,9},{11,... | collective-permute-start | bytes 393224 | tf_op jit(solution)/shard_map/ppermute | solution.py:37
  5.7 5.3 %collective-permute-start.4 = (f32[4,4,1920]{2,1,0:T(4,128)S(1)}, f32[4,4,1920]{2,1,0:T(4,128)S(1)}, u32[]{:S(2)}, u32[]{:S(2)}) collective-permute-start(f32[4,4,1920]{2,1,0:T(4,128)S(1)} %get-tuple-element.70), channel_id=1, source_target_pairs={{0,1},{1,0},{2,3},{3,2},{4,5},{5,4},{6,7},{7,6},{8,9},{9,8},{10,11... | collective-permute-start | bytes 368648 | tf_op jit(solution)/shard_map/ppermute | solution.py:37
  10.1 2.0 %collective-permute-start.3 = (f32[2,128]{1,0:T(2,128)S(1)}, f32[2,128]{1,0:T(2,128)S(1)}, u32[]{:S(2)}, u32[]{:S(2)}) collective-permute-start(f32[2,128]{1,0:T(2,128)S(1)} %relay.1.near), channel_id=1, source_target_pairs={{0,1},{1,0},{2,3},{3,2},{4,5},{5,4},{6,7},{7,6},{8,9},{9,8},{10,11... | collective-permute-start | bytes 3080 | tf_op jit(solution)/shard_map/ppermute | solution.py:37
  14.6 5.8 %collective-permute-start.5 = (f32[128]{0:T(128)S(1)}, f32[128]{0:T(128)S(1)}, u32[]{:S(2)}, u32[]{:S(2)}) collective-permute-start(f32[128]{0:T(128)S(1)} %bitcast.12), channel_id=1, source_target_pairs={{1,2},{2,1},{3,4},{4,3},{5,6},{6,5},{7,8},{8,7},{9,10},{10,9},{11,... | collective-permute-start | bytes 1544 | tf_op jit(solution)/shard_map/ppermute | solution.py:37
  15.3 5.1 %collective-permute-start.6 = (f32[128]{0:T(128)S(1)}, f32[128]{0:T(128)S(1)}, u32[]{:S(2)}, u32[]{:S(2)}) collective-permute-start(f32[128]{0:T(128)S(1)} %bitcast.11), channel_id=1, source_target_pairs={{0,1},{1,0},{2,3},{3,2},{4,5},{5,4},{6,7},{7,6},{8,9},{9,8},{10,11... | collective-permute-start | bytes 1544 | tf_op jit(solution)/shard_map/ppermute | solution.py:37
